TPU v7x, 32 devices: a whole 2x2x4 slice. The times are simulated.
32 devices in a mesh: groups: 2 (over x), mp: 16 (over z, y, core).
Axes of the slice: x: 2, y: 2, z: 4, core: 2. Of those that a mesh axis runs over, the one named last changes fastest.
Arguments:
- tokens: bfloat16 [2048, 8192], P('groups', 'mp'), parts along dimension 0, may hold values from -6 to 6
- up_blocks: bfloat16 [128, 8, 64, 512], P('mp'), may hold values from -0.25 to 0.25
- up_left: bfloat16 [8192, 256], P('mp'), may hold values from -0.0625 to 0.0625
- up_right: bfloat16 [256, 65536], P(None, 'mp'), may hold values from -0.375 to 0.375
- down_blocks: bfloat16 [128, 8, 512, 64], P('mp'), may hold values from -0.09375 to 0.09375
- down_left: bfloat16 [65536, 256], P('mp'), may hold values from -0.0234375 to 0.0234375
- down_right: bfloat16 [256, 8192], P(None, 'mp'), may hold values from -0.375 to 0.375
- cotangent: bfloat16 [2048, 8192], P('groups', 'mp'), parts along dimension 0, may hold values from -6 to 6
Outputs:
- output: bfloat16 [2048, 8192], P('groups', 'mp'), parts along dimension 0
- grad_tokens: bfloat16 [2048, 8192], P('groups', 'mp'), parts along dimension 0
- grad_up_blocks: float32 [256, 8, 64, 512], P(('groups', 'mp')), parts along dimension 0
- grad_up_left: float32 [16384, 256], P(('groups', 'mp')), parts along dimension 0
- grad_up_right: float32 [512, 65536], P('groups', 'mp'), parts along dimension 0
- grad_down_blocks: float32 [256, 8, 512, 64], P(('groups', 'mp')), parts along dimension 0
- grad_down_left: float32 [131072, 256], P(('groups', 'mp')), parts along dimension 0
- grad_down_right: float32 [512, 8192], P('groups', 'mp'), parts along dimension 0
There are 2 independent parts, one for each index of `groups`. A program takes and returns all parts, laid end to end along the dimension named above; an argument that names none is the same for every part. Nothing has to cross between parts.
All inputs are finite; a program needn't handle non-finite values.
Results may differ from a plain program's by a relative error of at most 0.0061.
Values may be sent and summed in bfloat16 or wider, within the bound.
A program may use at most 512 MiB of HBM per device.

v0:
```python
import jax
import jax.numpy as jnp
from jax import lax
from jax.sharding import PartitionSpec as P


def partner(block, axis, stride):
    count = lax.axis_size(axis)
    route = []
    for low in range(count):
        high = low | 1 << stride
        if high != low and high < count:
            route += [(low, high), (high, low)]
    return lax.ppermute(block, axis, route)


def gelu_value(field):
    inner = 0.7978845608 * (field + 0.044715 * field * field * field)
    return 0.5 * field * (1.0 + jnp.tanh(inner))


def gelu_slope(field):
    tangent = jnp.tanh(0.7978845608 * (field + 0.044715 * field * field * field))
    return 0.5 * (1.0 + tangent) + 0.5 * field * (1.0 - tangent * tangent) * 0.7978845608 * (
        1.0 + 3.0 * 0.044715 * field * field
    )


def flip_blocks(blocks, level):
    tok_rows, col_count, inner_width = blocks.shape
    split_view = blocks.reshape(tok_rows, col_count >> level + 1, 2, 1 << level, inner_width)
    return split_view[:, :, ::-1].reshape(tok_rows, col_count, inner_width)


def partner_pieces(own_blocks, ordering, swapper):
    return {level: swapper(own_blocks, level) for level in ordering}


def combine_terms(terms, local_bits, ordering, swapper):
    running = terms[0]
    for level in range(local_bits):
        running = running + flip_blocks(terms[1 + level], level)
    for level in ordering:
        running = running + swapper(terms[1 + local_bits + level], level)
    return running


def local(tokens, up_blocks, up_left, up_right, down_blocks, down_left, down_right, cotangent):
    tok_rows, feat_width = tokens.shape
    col_count, slot_count, row_block, col_block = up_blocks.shape
    local_bits = col_count.bit_length() - 1
    remote_bits = lax.axis_size("mp").bit_length() - 1
    ordering = list(range(remote_bits))
    own_inputs = tokens.reshape(tok_rows, col_count, row_block)
    own_cot = cotangent.reshape(tok_rows, col_count, row_block)
    far_inputs = partner_pieces(
        own_inputs, ordering, lambda portion, level: partner(portion, "mp", level)
    )
    low_a = lax.psum(jnp.dot(tokens, up_left, preferred_element_type=jnp.float32), "mp").astype(
        jnp.bfloat16
    )
    low_db = lax.psum(
        jnp.einsum("td,rd->tr", cotangent, down_right, preferred_element_type=jnp.float32), "mp"
    ).astype(jnp.bfloat16)
    far_cot = partner_pieces(
        own_cot, ordering, lambda portion, level: partner(portion, "mp", level)
    )
    input_slots = (
        [own_inputs]
        + [flip_blocks(own_inputs, level) for level in range(local_bits)]
        + [far_inputs[level] for level in range(remote_bits)]
    )
    hidden = jnp.zeros((tok_rows, col_count, col_block), jnp.float32)
    for slot_index in list(range(1 + local_bits)) + [1 + local_bits + level for level in ordering]:
        hidden = hidden + jnp.einsum(
            "tcd,cde->tce",
            input_slots[slot_index],
            up_blocks[:, slot_index],
            preferred_element_type=jnp.float32,
        )
    hidden = hidden.reshape(tok_rows, col_count * col_block) + jnp.dot(
        low_a, up_right, preferred_element_type=jnp.float32
    )
    act = gelu_value(hidden).astype(jnp.bfloat16)
    act_blocks = act.reshape(tok_rows, col_count, col_block)
    low_b = lax.psum(jnp.dot(act, down_left, preferred_element_type=jnp.float32), "mp").astype(
        jnp.bfloat16
    )
    down_terms = [
        jnp.einsum(
            "tce,ced->tcd",
            act_blocks,
            down_blocks[:, slot_index],
            preferred_element_type=jnp.float32,
        )
        for slot_index in range(slot_count)
    ]
    mixed = combine_terms(
        down_terms, local_bits, ordering, lambda portion, level: partner(portion, "mp", level)
    )
    output = (
        mixed.reshape(tok_rows, feat_width)
        + jnp.dot(low_b, down_right, preferred_element_type=jnp.float32)
    ).astype(jnp.bfloat16)
    grad_down_right = jnp.einsum("tr,td->rd", low_b, cotangent, preferred_element_type=jnp.float32)
    cot_slots = (
        [own_cot]
        + [flip_blocks(own_cot, level) for level in range(local_bits)]
        + [far_cot[level] for level in range(remote_bits)]
    )
    grad_act = jnp.zeros((tok_rows, col_count, col_block), jnp.float32)
    for slot_index in range(slot_count):
        grad_act = grad_act + jnp.einsum(
            "tcd,ced->tce",
            cot_slots[slot_index],
            down_blocks[:, slot_index],
            preferred_element_type=jnp.float32,
        )
    grad_down_blocks = jnp.stack(
        [
            jnp.einsum(
                "tce,tcd->ced",
                act_blocks,
                cot_slots[slot_index],
                preferred_element_type=jnp.float32,
            )
            for slot_index in range(slot_count)
        ],
        axis=1,
    )
    grad_down_left = jnp.einsum("th,tr->hr", act, low_db, preferred_element_type=jnp.float32)
    grad_act = grad_act.reshape(tok_rows, col_count * col_block) + jnp.einsum(
        "tr,hr->th", low_db, down_left, preferred_element_type=jnp.float32
    )
    grad_hidden = (grad_act * gelu_slope(hidden)).astype(jnp.bfloat16)
    grad_up_right = jnp.einsum("tr,th->rh", low_a, grad_hidden, preferred_element_type=jnp.float32)
    low_da = lax.psum(
        jnp.einsum("th,rh->tr", grad_hidden, up_right, preferred_element_type=jnp.float32), "mp"
    ).astype(jnp.bfloat16)
    hidden_blocks = grad_hidden.reshape(tok_rows, col_count, col_block)
    grad_up_blocks = jnp.stack(
        [
            jnp.einsum(
                "tcd,tce->cde",
                input_slots[slot_index],
                hidden_blocks,
                preferred_element_type=jnp.float32,
            )
            for slot_index in range(slot_count)
        ],
        axis=1,
    )
    back_terms = [
        jnp.einsum(
            "tce,cde->tcd",
            hidden_blocks,
            up_blocks[:, slot_index],
            preferred_element_type=jnp.float32,
        )
        for slot_index in range(slot_count)
    ]
    back_mixed = combine_terms(
        back_terms, local_bits, ordering, lambda portion, level: partner(portion, "mp", level)
    )
    grad_up_left = jnp.einsum("td,tr->dr", tokens, low_da, preferred_element_type=jnp.float32)
    grad_tokens = (
        back_mixed.reshape(tok_rows, feat_width)
        + jnp.einsum("tr,dr->td", low_da, up_left, preferred_element_type=jnp.float32)
    ).astype(jnp.bfloat16)
    return (
        output,
        grad_tokens,
        grad_up_blocks,
        grad_up_left,
        grad_up_right,
        grad_down_blocks,
        grad_down_left,
        grad_down_right,
    )


def solution(mesh):
    return jax.shard_map(
        local,
        mesh=mesh,
        in_specs=(
            P("groups", "mp"),
            P("mp", None, None, None),
            P("mp", None),
            P(None, "mp"),
            P("mp", None, None, None),
            P("mp", None),
            P(None, "mp"),
            P("groups", "mp"),
        ),
        out_specs=(
            P("groups", "mp"),
            P("groups", "mp"),
            P(("groups", "mp"), None, None, None),
            P(("groups", "mp"), None),
            P("groups", "mp"),
            P(("groups", "mp"), None, None, None),
            P(("groups", "mp"), None),
            P("groups", "mp"),
        ),
        check_vma=False,
    )
```

profile of v0, /device:TPU:0, one launch (start us, length us, event | category | flops | bytes accessed | tf_op | source)
XLA Modules:
  0.0 867.1 jit_solution(13038423592757179269)
XLA Ops:
  22.5 9.5 %fusion.244 = f32[8,512,1024]{2,1,0:T(8,128)} fusion(bf16[1024,8,64]{0,2,1:T(8,128)(2,1)} %bitcast.563, bf16[8,8,64,512]{3,2,1,0:T(8,128)(2,1)} %param.9), kind=kOutput, calls=%fused_computation.170 | convolution fusion | flops 536870912 | bytes 18350080 | tf_op jit(solution)/shard_map/tcd,cde->tce/dot_general | solution.py:75
  33.2 9.5 %fusion.247 = f32[8,512,1024]{2,1,0:T(8,128)} fusion(bf16[1024,8,64]{0,2,1:T(8,128)(2,1)} %bitcast.565, bf16[8,8,64,512]{3,2,1,0:T(8,128)(2,1)} %param.9), kind=kOutput, calls=%fused_computation.173 | convolution fusion | flops 536870912 | bytes 18350080 | tf_op jit(solution)/shard_map/tcd,cde->tce/dot_general | solution.py:75
  43.9 9.5 %fusion.250 = f32[8,512,1024]{2,1,0:T(8,128)} fusion(bf16[1024,8,64]{0,2,1:T(8,128)(2,1)} %bitcast.567, bf16[8,8,64,512]{3,2,1,0:T(8,128)(2,1)} %param.9), kind=kOutput, calls=%fused_computation.176 | convolution fusion | flops 536870912 | bytes 18350080 | tf_op jit(solution)/shard_map/tcd,cde->tce/dot_general | solution.py:75
  53.4 9.5 %fusion.226 = f32[8,512,1024]{2,1,0:T(8,128)} fusion(bf16[1024,8,64]{0,2,1:T(8,128)(2,1)} %bitcast.40, bf16[8,8,512,64]{2,3,1,0:T(8,128)(2,1)} %param.12), kind=kOutput, calls=%fused_computation.154 | convolution fusion | flops 536870912 | bytes 18350080 | tf_op jit(solution)/shard_map/tcd,ced->tce/dot_general | solution.py:113
  65.2 9.9 %fusion.217 = f32[8,512,1024]{2,1,0:T(8,128)} fusion(bf16[1024,8,64]{0,2,1:T(8,128)(2,1)} %bitcast.569, bf16[8,8,512,64]{2,3,1,0:T(8,128)(2,1)} %param.12), kind=kOutput, calls=%fused_computation.145 | convolution fusion | flops 536870912 | bytes 18350080 | tf_op jit(solution)/shard_map/tcd,ced->tce/dot_general | solution.py:113
  84.9 73.1 %all-reduce.4 = (bf16[1024,256]{1,0:T(8,128)(2,1)}, bf16[1024,256]{1,0:T(8,128)(2,1)}) all-reduce(f32[1024,256]{1,0:T(8,128)} %fusion.334, f32[1024,256]{1,0:T(8,128)} %fusion.336), channel_id=1, replica_groups=mesh['groups'=2,'mp'=16] {'mp'}, use_global_device_ids=true, to_apply=%region_0.0 | all-reduce | flops 524288 | bytes 3145728 | tf_op jit(solution)/shard_map/psum | solution.py:59
  158.0 9.4 %fusion.340 = f32[1024,4096]{1,0:T(8,128)} fusion(bf16[1024,256]{1,0:T(8,128)(2,1)} %get-tuple-element.27, bf16[4096,256]{1,0:T(8,128)(2,1)S(1)} %copy-done), kind=kOutput, calls=%fused_computation.266 | convolution fusion | flops 2147483648 | bytes 19398656 | tf_op jit(solution)/shard_map/tr,hr->th/dot_general | solution.py:132
  184.9 9.4 %fusion.223 = f32[8,512,1024]{2,1,0:T(8,128)} fusion(bf16[1024,8,64]{0,2,1:T(8,128)(2,1)S(1)} %bitcast.574, bf16[8,8,512,64]{2,3,1,0:T(8,128)(2,1)} %param.12), kind=kOutput, calls=%fused_computation.151 | convolution fusion | flops 536870912 | bytes 18350080 | tf_op jit(solution)/shard_map/tcd,ced->tce/dot_general | solution.py:113
  194.3 9.5 %fusion.235 = f32[8,512,1024]{2,1,0:T(8,128)} fusion(bf16[1024,8,64]{0,2,1:T(8,128)(2,1)} %collective-permute-done.2, bf16[8,8,64,512]{3,2,1,0:T(8,128)(2,1)S(1)} %copy-done.5), kind=kOutput, calls=%fused_computation.161 | convolution fusion | flops 536870912 | bytes 18350080 | tf_op jit(solution)/shard_map/tcd,cde->tce/dot_general | solution.py:75
  203.8 20.4 %fusion.238 = f32[8,512,1024]{2,1,0:T(8,128)} fusion(bf16[1024,8,64]{0,2,1:T(8,128)(2,1)} %collective-permute-done.1, bf16[8,8,64,512]{3,2,1,0:T(8,128)(2,1)S(1)} %copy-done.5), kind=kOutput, calls=%fused_computation.164 | convolution fusion | flops 536870912 | bytes 18350080 | tf_op jit(solution)/shard_map/tcd,cde->tce/dot_general | solution.py:75
  224.3 9.5 %fusion.241 = f32[8,512,1024]{2,1,0:T(8,128)} fusion(bf16[1024,8,64]{0,2,1:T(8,128)(2,1)} %collective-permute-done, bf16[8,8,64,512]{3,2,1,0:T(8,128)(2,1)S(1)} %copy-done.5), kind=kOutput, calls=%fused_computation.167 | convolution fusion | flops 536870912 | bytes 18350080 | tf_op jit(solution)/shard_map/tcd,cde->tce/dot_general | solution.py:75
  233.8 38.9 %add_add_fusion.1 = f32[8,512,1024]{2,1,0:T(8,128)} fusion(f32[8,512,1024]{2,1,0:T(8,128)} %fusion.235, f32[8,512,1024]{2,1,0:T(8,128)} %fusion.238, f32[8,512,1024]{2,1,0:T(8,128)} %fusion.241, f32[8,512,1024]{2,1,0:T(8,128)} %fusion.244, f32[8,512,1024]{2,1,0:T(8,128)} %fusion.247, f32[8,512,1024]{2,1,0:T(8,128)S(1)} %bitcast.511, ...), kind=kOutput, calls=%fused_computation.10 | convolution fusion | flops 566231040 | bytes 135790592 | tf_op jit(solution)/shard_map/tcd,cde->tce/dot_general | solution.py:75
  272.7 17.5 %copy.91 = f32[1024,4096]{1,0:T(8,128)} copy(f32[1024,4096]{0,1:T(8,128)} %bitcast.532) | data formatting | bytes 33554432 | tf_op jit(solution)/shard_map/reshape | solution.py:81
  290.2 9.5 %fusion.208 = f32[8,512,1024]{2,1,0:T(8,128)} fusion(bf16[1024,8,64]{0,2,1:T(8,128)(2,1)} %collective-permute-done.10, bf16[8,8,512,64]{2,3,1,0:T(8,128)(2,1)} %param.12), kind=kOutput, calls=%fused_computation.136 | convolution fusion | flops 536870912 | bytes 18350080 | tf_op jit(solution)/shard_map/tcd,ced->tce/dot_general | solution.py:113
  299.8 9.6 %fusion.211 = f32[8,512,1024]{2,1,0:T(8,128)} fusion(bf16[1024,8,64]{0,2,1:T(8,128)(2,1)} %collective-permute-done.9, bf16[8,8,512,64]{2,3,1,0:T(8,128)(2,1)} %param.12), kind=kOutput, calls=%fused_computation.139 | convolution fusion | flops 536870912 | bytes 18350080 | tf_op jit(solution)/shard_map/tcd,ced->tce/dot_general | solution.py:113
  309.4 9.7 %fusion.214 = f32[8,512,1024]{2,1,0:T(8,128)} fusion(bf16[1024,8,64]{0,2,1:T(8,128)(2,1)} %collective-permute-done.8, bf16[8,8,512,64]{2,3,1,0:T(8,128)(2,1)} %param.12), kind=kOutput, calls=%fused_computation.142 | convolution fusion | flops 536870912 | bytes 18350080 | tf_op jit(solution)/shard_map/tcd,ced->tce/dot_general | solution.py:113
  319.2 38.9 %add_add_fusion = f32[8,512,1024]{2,1,0:T(8,128)} fusion(f32[8,512,1024]{2,1,0:T(8,128)} %fusion.208, f32[8,512,1024]{2,1,0:T(8,128)} %fusion.211, f32[8,512,1024]{2,1,0:T(8,128)} %fusion.214, f32[8,512,1024]{2,1,0:T(8,128)} %fusion.217, f32[8,512,1024]{2,1,0:T(8,128)} %fusion.220, f32[8,512,1024]{2,1,0:T(8,128)S(1)} %bitcast.509, ...), kind=kOutput, calls=%fused_computation.9 | convolution fusion | flops 566231040 | bytes 135790592 | tf_op jit(solution)/shard_map/tcd,ced->tce/dot_general | solution.py:113
  358.1 17.5 %copy.142 = f32[1024,4096]{1,0:T(8,128)} copy(f32[1024,4096]{0,1:T(8,128)} %bitcast.533) | data formatting | bytes 33554432 | tf_op jit(solution)/shard_map/reshape | solution.py:132
  375.6 30.1 %fusion.6 = (bf16[1024,4096]{1,0:T(8,128)(2,1)}, bf16[1024,4096]{1,0:T(8,128)(2,1)}) fusion(f32[1024,4096]{1,0:T(8,128)} %copy.142, f32[1024,4096]{1,0:T(8,128)} %fusion.340, f32[1024,4096]{1,0:T(8,128)} %copy.91, f32[1024,4096]{1,0:T(8,128)} %fusion.344), kind=kLoop, calls=%fused_computation.8 | loop fusion | flops 96468992 | bytes 83886080 | tf_op jit(solution)/shard_map/convert_element_type | solution.py:135
  503.5 156.4 %all-reduce.5 = (bf16[1024,256]{1,0:T(8,128)(2,1)}, bf16[1024,256]{1,0:T(8,128)(2,1)S(1)}) all-reduce(f32[1024,256]{1,0:T(8,128)} %fusion.335, f32[1024,256]{1,0:T(8,128)} %fusion.337), channel_id=1, replica_groups=mesh['groups'=2,'mp'=16] {'mp'}, use_global_device_ids=true, to_apply=%region_1.0 | all-reduce | flops 524288 | bytes 3145728 | tf_op jit(solution)/shard_map/psum | solution.py:86
  762.7 11.3 %fusion.78 = f32[1024,8,64]{0,2,1:T(8,128)} fusion(f32[1024,8,64]{0,2,1:T(8,128)} %collective-permute-done.7, f32[1024,8,64]{0,2,1:T(8,128)} %collective-permute-done.6, f32[1024,8,64]{0,2,1:T(8,128)} %collective-permute-done.5, f32[1024,8,64]{0,2,1:T(8,128)} %collective-permute-done.4, f32[1024,1,2,4,64]{0,4,3,2,1:T(8,128)} %rev.41, ...), kind=kOutput, calls=%fused_computation.87 | convolution fusion | flops 540540928 | bytes 25690112 | tf_op jit(solution)/shard_map/tce,ced->tcd/dot_general | solution.py:90
  777.2 22.8 %collective-permute-done.13 = f32[1024,8,64]{0,2,1:T(8,128)} collective-permute-done((f32[1024,8,64]{0,2,1:T(8,128)}, f32[1024,8,64]{0,2,1:T(8,128)}, u32[]{:S(2)}, u32[]{:S(2)}) %collective-permute-start.13) | collective-permute-done | bytes 2097184 | tf_op jit(solution)/shard_map/ppermute | solution.py:14
  800.0 42.8 %collective-permute-done.14 = f32[1024,8,64]{0,2,1:T(8,128)} collective-permute-done((f32[1024,8,64]{0,2,1:T(8,128)}, f32[1024,8,64]{0,2,1:T(8,128)}, u32[]{:S(2)}, u32[]{:S(2)}) %collective-permute-start.14) | collective-permute-done | bytes 2097184 | tf_op jit(solution)/shard_map/ppermute | solution.py:14
  846.0 12.3 %fusion.74 = f32[1024,8,64]{0,2,1:T(8,128)} fusion(f32[1024,8,64]{0,2,1:T(8,128)} %collective-permute-done.15, f32[1024,8,64]{0,2,1:T(8,128)} %collective-permute-done.14, f32[1024,8,64]{0,2,1:T(8,128)} %collective-permute-done.13, f32[1024,8,64]{0,2,1:T(8,128)} %collective-permute-done.12, f32[1024,1,2,4,64]{0,4,3,2,1:T(8,128)} %rev.47, ...), kind=kOutput, calls=%fused_computation.80 | convolution fusion | flops 540540928 | bytes 25690112 | tf_op jit(solution)/shard_map/tce,cde->tcd/dot_general | solution.py:154
  (176 shorter events, 269.3 us)
Async XLA Ops:
  0.6 157.4 %copy-start = (bf16[4096,256]{1,0:T(8,128)(2,1)S(1)}, bf16[4096,256]{1,0:T(8,128)(2,1)}, u32[]{:S(2)}) copy-start(bf16[4096,256]{1,0:T(8,128)(2,1)} %param.13) | copy-start | bytes 6291460
  2.3 40.4 %copy-start.1 = (bf16[1024,512]{0,1:T(8,128)(2,1)}, bf16[1024,512]{0,1:T(8,128)(2,1)S(1)}, u32[]{:S(2)}) copy-start(bf16[1024,512]{0,1:T(8,128)(2,1)S(1)} %copy.80) | copy-start | bytes 3145732
  2.3 192.0 %collective-permute-start.2 = (bf16[1024,8,64]{0,2,1:T(8,128)(2,1)S(1)}, bf16[1024,8,64]{0,2,1:T(8,128)(2,1)}, u32[]{:S(2)}, u32[]{:S(2)}) collective-permute-start(bf16[1024,8,64]{0,2,1:T(8,128)(2,1)S(1)} %bitcast.534), channel_id=1, source_target_pairs={{0,4},{4,0},{1,5},{5,1},{2,6},{6,2},{3,7},{7,3},{8,12},{12,8},{9,1... | collective-permute-start | bytes 3145736 | tf_op jit(solution)/shard_map/ppermute | solution.py:14
  5.4 198.4 %collective-permute-start.1 = (bf16[1024,8,64]{0,2,1:T(8,128)(2,1)S(1)}, bf16[1024,8,64]{0,2,1:T(8,128)(2,1)}, u32[]{:S(2)}, u32[]{:S(2)}) collective-permute-start(bf16[1024,8,64]{0,2,1:T(8,128)(2,1)S(1)} %bitcast.535), channel_id=1, source_target_pairs={{0,2},{2,0},{1,3},{3,1},{4,6},{6,4},{5,7},{7,5},{8,10},{10,8},{9,1... | collective-permute-start | bytes 3145736 | tf_op jit(solution)/shard_map/ppermute | solution.py:14
  6.9 217.3 %collective-permute-start = (bf16[1024,8,64]{0,2,1:T(8,128)(2,1)S(1)}, bf16[1024,8,64]{0,2,1:T(8,128)(2,1)}, u32[]{:S(2)}, u32[]{:S(2)}) collective-permute-start(bf16[1024,8,64]{0,2,1:T(8,128)(2,1)S(1)} %bitcast.536), channel_id=1, source_target_pairs={{0,1},{1,0},{2,3},{3,2},{4,5},{5,4},{6,7},{7,6},{8,9},{9,8},{10,11... | collective-permute-start | bytes 3145736 | tf_op jit(solution)/shard_map/ppermute | solution.py:14
  6.9 226.9 %collective-permute-start.3 = (bf16[1024,8,64]{0,2,1:T(8,128)(2,1)S(1)}, bf16[1024,8,64]{0,2,1:T(8,128)(2,1)}, u32[]{:S(2)}, u32[]{:S(2)}) collective-permute-start(bf16[1024,8,64]{0,2,1:T(8,128)(2,1)S(1)} %bitcast.537), channel_id=1, source_target_pairs={{0,8},{8,0},{1,9},{9,1},{2,10},{10,2},{3,11},{11,3},{4,12},{12,4},... | collective-permute-start | bytes 3145736 | tf_op jit(solution)/shard_map/ppermute | solution.py:14
  11.8 278.5 %collective-permute-start.10 = (bf16[1024,8,64]{0,2,1:T(8,128)(2,1)}, bf16[1024,8,64]{0,2,1:T(8,128)(2,1)}, u32[]{:S(2)}, u32[]{:S(2)}) collective-permute-start(bf16[1024,8,64]{0,2,1:T(8,128)(2,1)} %bitcast.40), channel_id=1, source_target_pairs={{0,4},{4,0},{1,5},{5,1},{2,6},{6,2},{3,7},{7,3},{8,12},{12,8},{9,1... | collective-permute-start | bytes 3145736 | tf_op jit(solution)/shard_map/ppermute | solution.py:14
  65.2 14.4 %copy-start.21 = (bf16[512,256]{1,0:T(8,128)(2,1)S(1)}, bf16[512,256]{1,0:T(8,128)(2,1)}, u32[]{:S(2)}) copy-start(bf16[512,256]{1,0:T(8,128)(2,1)} %param.10) | copy-start | bytes 786436
  194.3 105.5 %collective-permute-start.9 = (bf16[1024,8,64]{0,2,1:T(8,128)(2,1)}, bf16[1024,8,64]{0,2,1:T(8,128)(2,1)}, u32[]{:S(2)}, u32[]{:S(2)}) collective-permute-start(bf16[1024,8,64]{0,2,1:T(8,128)(2,1)} %bitcast.40), channel_id=1, source_target_pairs={{0,2},{2,0},{1,3},{3,1},{4,6},{6,4},{5,7},{7,5},{8,10},{10,8},{9,1... | collective-permute-start | bytes 3145736 | tf_op jit(solution)/shard_map/ppermute | solution.py:14
  203.8 105.6 %collective-permute-start.8 = (bf16[1024,8,64]{0,2,1:T(8,128)(2,1)}, bf16[1024,8,64]{0,2,1:T(8,128)(2,1)}, u32[]{:S(2)}, u32[]{:S(2)}) collective-permute-start(bf16[1024,8,64]{0,2,1:T(8,128)(2,1)} %bitcast.40), channel_id=1, source_target_pairs={{0,1},{1,0},{2,3},{3,2},{4,5},{5,4},{6,7},{7,6},{8,9},{9,8},{10,11... | collective-permute-start | bytes 3145736 | tf_op jit(solution)/shard_map/ppermute | solution.py:14
  203.8 30.0 %slice-start.4 = ((s8[16777216]{0:T(1024)(128)(4,1)}), s8[4194304]{0:T(1024)(128)(4,1)S(1)}, s32[]{:S(2)}) async-start(s8[16777216]{0:T(1024)(128)(4,1)} %bitcast.510), calls=%async_computation.4 | async-start | bytes 8388608
  203.8 30.0 %slice-start.5 = ((s8[16777216]{0:T(1024)(128)(4,1)}), s8[4194304]{0:T(1024)(128)(4,1)S(1)}, s32[]{:S(2)}) async-start(s8[16777216]{0:T(1024)(128)(4,1)} %bitcast.510), calls=%async_computation.5 | async-start | bytes 8388608
  224.2 94.9 %collective-permute-start.11 = (bf16[1024,8,64]{0,2,1:T(8,128)(2,1)}, bf16[1024,8,64]{0,2,1:T(8,128)(2,1)}, u32[]{:S(2)}, u32[]{:S(2)}) collective-permute-start(bf16[1024,8,64]{0,2,1:T(8,128)(2,1)} %bitcast.40), channel_id=1, source_target_pairs={{0,8},{8,0},{1,9},{9,1},{2,10},{10,2},{3,11},{11,3},{4,12},{12,4},... | collective-permute-start | bytes 3145736 | tf_op jit(solution)/shard_map/ppermute | solution.py:14
  299.8 19.4 %slice-start = ((s8[16777216]{0:T(1024)(128)(4,1)}), s8[4194304]{0:T(1024)(128)(4,1)S(1)}, s32[]{:S(2)}) async-start(s8[16777216]{0:T(1024)(128)(4,1)} %bitcast.508), calls=%async_computation | async-start | bytes 8388608
  299.8 19.4 %slice-start.1 = ((s8[16777216]{0:T(1024)(128)(4,1)}), s8[4194304]{0:T(1024)(128)(4,1)S(1)}, s32[]{:S(2)}) async-start(s8[16777216]{0:T(1024)(128)(4,1)} %bitcast.508), calls=%async_computation.1 | async-start | bytes 8388608
  498.5 253.1 %collective-permute-start.4 = (f32[1024,8,64]{0,2,1:T(8,128)}, f32[1024,8,64]{0,2,1:T(8,128)}, u32[]{:S(2)}, u32[]{:S(2)}) collective-permute-start(f32[1024,8,64]{0,2,1:T(8,128)} %fusion.81), channel_id=1, source_target_pairs={{0,1},{1,0},{2,3},{3,2},{4,5},{5,4},{6,7},{7,6},{8,9},{9,8},{10,11... | collective-permute-start | bytes 6291464 | tf_op jit(solution)/shard_map/ppermute | solution.py:14
  499.0 252.6 %collective-permute-start.5 = (f32[1024,8,64]{0,2,1:T(8,128)}, f32[1024,8,64]{0,2,1:T(8,128)}, u32[]{:S(2)}, u32[]{:S(2)}) collective-permute-start(f32[1024,8,64]{0,2,1:T(8,128)} %fusion.84), channel_id=1, source_target_pairs={{0,2},{2,0},{1,3},{3,1},{4,6},{6,4},{5,7},{7,5},{8,10},{10,8},{9,1... | collective-permute-start | bytes 6291464 | tf_op jit(solution)/shard_map/ppermute | solution.py:14
  501.0 250.7 %collective-permute-start.6 = (f32[1024,8,64]{0,2,1:T(8,128)}, f32[1024,8,64]{0,2,1:T(8,128)}, u32[]{:S(2)}, u32[]{:S(2)}) collective-permute-start(f32[1024,8,64]{0,2,1:T(8,128)} %fusion.87), channel_id=1, source_target_pairs={{0,4},{4,0},{1,5},{5,1},{2,6},{6,2},{3,7},{7,3},{8,12},{12,8},{9,1... | collective-permute-start | bytes 6291464 | tf_op jit(solution)/shard_map/ppermute | solution.py:14
  501.0 261.7 %collective-permute-start.7 = (f32[1024,8,64]{0,2,1:T(8,128)}, f32[1024,8,64]{0,2,1:T(8,128)}, u32[]{:S(2)}, u32[]{:S(2)}) collective-permute-start(f32[1024,8,64]{0,2,1:T(8,128)} %fusion.90), channel_id=1, source_target_pairs={{0,8},{8,0},{1,9},{9,1},{2,10},{10,2},{3,11},{11,3},{4,12},{12,4},... | collective-permute-start | bytes 6291464 | tf_op jit(solution)/shard_map/ppermute | solution.py:14
  727.0 13.9 %copy-start.23 = (bf16[256,512]{1,0:T(8,128)(2,1)S(1)}, bf16[256,512]{1,0:T(8,128)(2,1)}, u32[]{:S(2)}) copy-start(bf16[256,512]{1,0:T(8,128)(2,1)} %param.14) | copy-start | bytes 786436
  730.2 46.9 %collective-permute-start.12 = (f32[1024,8,64]{0,2,1:T(8,128)}, f32[1024,8,64]{0,2,1:T(8,128)}, u32[]{:S(2)}, u32[]{:S(2)}) collective-permute-start(f32[1024,8,64]{0,2,1:T(8,128)} %fusion.95), channel_id=1, source_target_pairs={{0,1},{1,0},{2,3},{3,2},{4,5},{5,4},{6,7},{7,6},{8,9},{9,8},{10,11... | collective-permute-start | bytes 6291464 | tf_op jit(solution)/shard_map/ppermute | solution.py:14
  751.7 48.3 %collective-permute-start.13 = (f32[1024,8,64]{0,2,1:T(8,128)}, f32[1024,8,64]{0,2,1:T(8,128)}, u32[]{:S(2)}, u32[]{:S(2)}) collective-permute-start(f32[1024,8,64]{0,2,1:T(8,128)} %fusion.98), channel_id=1, source_target_pairs={{0,2},{2,0},{1,3},{3,1},{4,6},{6,4},{5,7},{7,5},{8,10},{10,8},{9,1... | collective-permute-start | bytes 6291464 | tf_op jit(solution)/shard_map/ppermute | solution.py:14
  751.7 91.1 %collective-permute-start.14 = (f32[1024,8,64]{0,2,1:T(8,128)}, f32[1024,8,64]{0,2,1:T(8,128)}, u32[]{:S(2)}, u32[]{:S(2)}) collective-permute-start(f32[1024,8,64]{0,2,1:T(8,128)} %fusion.101), channel_id=1, source_target_pairs={{0,4},{4,0},{1,5},{5,1},{2,6},{6,2},{3,7},{7,3},{8,12},{12,8},{9,1... | collective-permute-start | bytes 6291464 | tf_op jit(solution)/shard_map/ppermute | solution.py:14
  751.8 94.3 %collective-permute-start.15 = (f32[1024,8,64]{0,2,1:T(8,128)}, f32[1024,8,64]{0,2,1:T(8,128)}, u32[]{:S(2)}, u32[]{:S(2)}) collective-permute-start(f32[1024,8,64]{0,2,1:T(8,128)} %fusion.104), channel_id=1, source_target_pairs={{0,8},{8,0},{1,9},{9,1},{2,10},{10,2},{3,11},{11,3},{4,12},{12,4},... | collective-permute-start | bytes 6291464 | tf_op jit(solution)/shard_map/ppermute | solution.py:14
  (31 other events, 237.3 us)
where the time goes:
time: 878 us; the launch traced here: 867 us
  matrix products  424 us (48%)
  blocking collectives  229 us (26%)
  local copies, waits for them, and re-layouts  92.9 us (11%)
  waiting for transfers between devices  68.9 us (8%)
  other arithmetic  35.6 us (4%)
  starting transfers between devices  14.5 us (2%)
    psum x1, blocking collectives, local(): lax.psum(jnp.dot(act, down_left, preferred_element_type=jnp.float32), 'mp')  156 us
    dot_general x8, matrix products, local(): jnp.einsum('tcd,cde->tce', input_slots[slot_index], up_blocks[:, slot_ind...  116 us
    dot_general x8, matrix products, local(): jnp.einsum('tcd,ced->tce', cot_slots[slot_index], down_blocks[:, slot_ind...  106 us
    psum x1, blocking collectives, local(): lax.psum(jnp.dot(tokens, up_left, preferred_element_type=jnp.float32), 'mp')  73.1 us
    ppermute x16, waiting for transfers between devices, partner(): return lax.ppermute(block, axis, route)  68.9 us
    dot_general x8, matrix products, local(): jnp.einsum('tce,cde->tcd', hidden_blocks, up_blocks[:, slot_index], prefe...  47.8 us
    dot_general x8, matrix products, local(): jnp.einsum('tce,ced->tcd', act_blocks, down_blocks[:, slot_index], prefer...  40.7 us
    dot_general x8, matrix products, local(): jnp.einsum('tce,tcd->ced', act_blocks, cot_slots[slot_index], preferred_e...  36.2 us
  transfers between devices with their start and end apart: 16, of which 3 were waited for; matrix products, arithmetic and copies ran while one was open for 41% of the time, Pallas kernels for 0%

commit v1 on v0

v1 whole, which is shorter than its diff:
```python
import functools

import jax
import jax.numpy as jnp
from jax import lax
from jax.experimental import pallas as pl
from jax.experimental.pallas import tpu as pltpu
from jax.sharding import PartitionSpec as P

CHUNKS = 2
TILE = 256
VMEM_BYTES = 48 * 1024 * 1024


def partner(block, axis, stride):
    count = lax.axis_size(axis)
    route = []
    for low in range(count):
        high = low | 1 << stride
        if high != low and high < count:
            route += [(low, high), (high, low)]
    return lax.ppermute(block, axis, route)


def gelu_both(field):
    square = field * field
    tangent = jnp.tanh(field * (0.7978845608 + 0.7978845608 * 0.044715 * square))
    half = 0.5 + 0.5 * tangent
    slope = half + 0.5 * field * (1.0 - tangent * tangent) * (
        0.7978845608 + 0.7978845608 * 3.0 * 0.044715 * square
    )
    return field * half, slope


def mul(left, right, left_dim, right_dim):
    return lax.dot_general(
        left, right, (((left_dim,), (right_dim,)), ((), ())), preferred_element_type=jnp.float32
    )


def middle_kernel(local_bits, remote_bits, *refs):
    slots = 1 + local_bits + remote_bits
    pieces = refs[:slots]
    up_ref, down_ref, right_ref, left_ref, low_ref = refs[slots : slots + 5]
    act_ref, grad_ref, near_ref, sums_ref = refs[slots + 5 : slots + 9]
    fars = refs[slots + 9 :]
    column = pl.program_id(0)

    @pl.when(column == 0)
    def _():
        near_ref[...] = jnp.zeros_like(near_ref)
        sums_ref[...] = jnp.zeros_like(sums_ref)

    rank = right_ref.shape[0]
    rows = pieces[0].shape[2]
    width = pieces[0].shape[3]
    tile = min(TILE, width)
    up = up_ref[0]
    down = down_ref[0]
    right = right_ref[...]
    left = left_ref[...]
    for start in range(0, width, tile):
        span = pl.ds(start, tile)
        x = jnp.concatenate([piece[0, 0, :, span] for piece in pieces], axis=0)
        c = jnp.concatenate([piece[1, 0, :, span] for piece in pieces], axis=0)
        hidden = mul(up, x, 0, 0) + mul(right, low_ref[:rank, span], 0, 0)
        grad_act = mul(down, c, 0, 0) + mul(left, low_ref[rank:, span], 1, 0)
        value, slope = gelu_both(hidden)
        act = value.astype(jnp.bfloat16)
        grad = (grad_act * slope).astype(jnp.bfloat16)
        act_ref[0, :, span] = act
        grad_ref[0, :, span] = grad
        sums_ref[:rank, span] += mul(left, act, 0, 0)
        sums_ref[rank:, span] += mul(right, grad, 1, 0)
        for side, (weight, field) in enumerate(((down, act), (up, grad))):
            terms = mul(weight, field, 1, 0)
            for slot in range(slots):
                term = terms[slot * rows : (slot + 1) * rows]
                if slot <= local_bits:
                    target = column ^ ((1 << slot) >> 1)
                    near_ref[side, target, :, span] += term
                else:
                    fars[slot - 1 - local_bits][side, 0, :, span] = term.astype(jnp.bfloat16)


def grad_kernel(chunks, slots, *refs):
    pieces = [refs[part * slots : (part + 1) * slots] for part in range(chunks)]
    rest = refs[chunks * slots :]
    acts, grads, lows = rest[:chunks], rest[chunks : 2 * chunks], rest[2 * chunks : 3 * chunks]
    up_ref, down_ref, right_ref, left_ref = rest[3 * chunks :]
    rank = right_ref.shape[0]

    def total(terms):
        return functools.reduce(lambda one, two: one + two, terms)

    up_ref[0] = total(
        mul(jnp.concatenate([piece[0, 0] for piece in pieces[part]], axis=0), grads[part][0], 1, 1)
        for part in range(chunks)
    )
    down_ref[0] = total(
        mul(jnp.concatenate([piece[1, 0] for piece in pieces[part]], axis=0), acts[part][0], 1, 1)
        for part in range(chunks)
    )
    right_ref[...] = total(
        mul(lows[part][:rank], grads[part][0], 1, 1) for part in range(chunks)
    )
    left_ref[...] = total(
        mul(acts[part][0], lows[part][rank:], 1, 1) for part in range(chunks)
    )


def local(tokens, up_blocks, up_left, up_right, down_blocks, down_left, down_right, cotangent):
    tok_rows, feat_width = tokens.shape
    col_count, slots, rows, col_block = up_blocks.shape
    rank = up_left.shape[1]
    local_bits = col_count.bit_length() - 1
    remote_bits = lax.axis_size("mp").bit_length() - 1
    deep = slots * rows
    part = tok_rows // CHUNKS
    up = up_blocks.reshape(col_count, deep, col_block)
    down = down_blocks.swapaxes(2, 3).reshape(col_count, deep, col_block)
    both = jnp.stack([tokens.T, cotangent.T])
    mine = [
        both[:, :, start : start + part].reshape(2, col_count, rows, part)
        for start in range(0, tok_rows, part)
    ]

    def shared_sum(total):
        piece = lax.psum_scatter(total, "mp", scatter_dimension=0, tiled=True)
        return lax.all_gather(piece.astype(jnp.bfloat16), "mp", axis=0, tiled=True)

    low = shared_sum(
        jnp.concatenate(
            [
                jnp.einsum("dr,dt->rt", up_left, both[0], preferred_element_type=jnp.float32),
                jnp.einsum("rd,dt->rt", down_right, both[1], preferred_element_type=jnp.float32),
            ]
        )
    )
    lows = [low[:, start : start + part] for start in range(0, tok_rows, part)]

    own_specs = [
        pl.BlockSpec((2, 1, rows, part), lambda j, m=(1 << slot) >> 1: (0, j ^ m, 0, 0))
        for slot in range(1 + local_bits)
    ]
    far_spec = pl.BlockSpec((2, 1, rows, part), lambda j: (0, j, 0, 0))
    piece_specs = own_specs + [far_spec] * remote_bits
    block_spec = pl.BlockSpec((1, deep, col_block), lambda j: (j, 0, 0))
    field_spec = pl.BlockSpec((1, col_block, part), lambda j: (j, 0, 0))
    right_spec = pl.BlockSpec((rank, col_block), lambda j: (0, j))
    left_spec = pl.BlockSpec((col_block, rank), lambda j: (j, 0))
    low_spec = pl.BlockSpec((2 * rank, part), lambda j: (0, 0))
    field = jax.ShapeDtypeStruct((col_count, col_block, part), jnp.bfloat16)
    hidden_units = col_count * col_block
    params = pltpu.CompilerParams(vmem_limit_bytes=VMEM_BYTES)
    flops = 2 * tok_rows * hidden_units * (deep + rank)
    middle = pl.pallas_call(
        functools.partial(middle_kernel, local_bits, remote_bits),
        grid=(col_count,),
        in_specs=piece_specs + [block_spec, block_spec, right_spec, left_spec, low_spec],
        out_specs=[
            field_spec,
            field_spec,
            pl.BlockSpec((2, col_count, rows, part), lambda j: (0, 0, 0, 0)),
            low_spec,
        ]
        + [far_spec] * remote_bits,
        out_shape=[
            field,
            field,
            jax.ShapeDtypeStruct((2, col_count, rows, part), jnp.float32),
            jax.ShapeDtypeStruct((2 * rank, part), jnp.float32),
        ]
        + [jax.ShapeDtypeStruct((2, col_count, rows, part), jnp.bfloat16)] * remote_bits,
        compiler_params=params,
        cost_estimate=pl.CostEstimate(
            flops=4 * flops // CHUNKS,
            bytes_accessed=64 * hidden_units * part // 8,
            transcendentals=hidden_units * part,
        ),
    )
    pieces, fields, grads, nears, sums, far_terms = [], [], [], [], [], []
    for index in range(CHUNKS):
        far = [partner(mine[index], "mp", level) for level in reversed(range(remote_bits))][::-1]
        pieces.append([mine[index]] * (1 + local_bits) + far)
    for index in range(CHUNKS):
        act, grad, near, total, *terms = middle(
            *pieces[index], up, down, up_right, down_left, lows[index]
        )
        far_terms.append(
            [partner(terms[level], "mp", level) for level in reversed(range(remote_bits))]
        )
        sums.append(shared_sum(total))
        fields.append(act)
        grads.append(grad)
        nears.append(near)

    grad_up, grad_down, grad_up_right, grad_down_left = pl.pallas_call(
        functools.partial(grad_kernel, CHUNKS, slots),
        grid=(col_count,),
        in_specs=piece_specs * CHUNKS + [field_spec] * (2 * CHUNKS) + [low_spec] * CHUNKS,
        out_specs=[block_spec, block_spec, right_spec, left_spec],
        out_shape=[
            jax.ShapeDtypeStruct((col_count, deep, col_block), jnp.float32),
            jax.ShapeDtypeStruct((col_count, deep, col_block), jnp.float32),
            jax.ShapeDtypeStruct(up_right.shape, jnp.float32),
            jax.ShapeDtypeStruct(down_left.shape, jnp.float32),
        ],
        compiler_params=params,
        cost_estimate=pl.CostEstimate(
            flops=2 * flops, bytes_accessed=16 * hidden_units * tok_rows, transcendentals=0
        ),
    )(*[piece for group in pieces for piece in group], *fields, *grads, *lows)

    results = []
    for index in range(CHUNKS):
        mixed = nears[index]
        for term in far_terms[index]:
            mixed = mixed + term.astype(jnp.float32)
        mixed = mixed.reshape(2, feat_width, part)
        back = jnp.stack(
            [
                jnp.einsum(
                    "rd,rt->dt", down_right, sums[index][:rank], preferred_element_type=jnp.float32
                ),
                jnp.einsum(
                    "dr,rt->dt", up_left, sums[index][rank:], preferred_element_type=jnp.float32
                ),
            ]
        )
        results.append((mixed + back).astype(jnp.bfloat16))
    result = jnp.concatenate(results, axis=2)
    total = jnp.concatenate(sums, axis=1)
    grad_down_right = jnp.einsum(
        "rt,dt->rd", total[:rank], both[1], preferred_element_type=jnp.float32
    )
    grad_up_left = jnp.einsum(
        "dt,rt->dr", both[0], total[rank:], preferred_element_type=jnp.float32
    )
    return (
        result[0].T,
        result[1].T,
        grad_up.reshape(up_blocks.shape),
        grad_up_left,
        grad_up_right,
        grad_down.reshape(col_count, slots, rows, col_block).swapaxes(2, 3),
        grad_down_left,
        grad_down_right,
    )


def solution(mesh):
    return jax.shard_map(
        local,
        mesh=mesh,
        in_specs=(
            P("groups", "mp"),
            P("mp", None, None, None),
            P("mp", None),
            P(None, "mp"),
            P("mp", None, None, None),
            P("mp", None),
            P(None, "mp"),
            P("groups", "mp"),
        ),
        out_specs=(
            P("groups", "mp"),
            P("groups", "mp"),
            P(("groups", "mp"), None, None, None),
            P(("groups", "mp"), None),
            P("groups", "mp"),
            P(("groups", "mp"), None, None, None),
            P(("groups", "mp"), None),
            P("groups", "mp"),
        ),
        check_vma=False,
    )
```

time: 878 us -> 391 us (0.45); the launches traced: 867 us -> 391 us
  matrix products: 424 us -> 9.89 us
  blocking collectives: 229 us -> 41 us
  waiting for transfers between devices: 68.9 us -> 199 us
  Pallas kernels: 0 us -> 71 us
  local copies, waits for them, and re-layouts: 92.9 us -> 22 us
  other arithmetic: 35.6 us -> 18.9 us
  between operations: 1.34 us -> 14 us
    dot_general x60 -> x8, matrix products: 424 us -> 9.89 us  [the longest x2 2.64 us: local(): jnp.einsum('dr,rt->dt', up_left, sums[index][rank:], preferred_element_ty...]
    psum x2 -> x0, blocking collectives: 229 us -> none  [the longest x1 156 us: local(): lax.psum(jnp.dot(act, down_left, preferred_element_type=jnp.float32), 'mp')]
    reduce_scatter x0 -> x3, waiting for transfers between devices: none -> 96.2 us  [shared_sum(): piece = lax.psum_scatter(total, 'mp', scatter_dimension=0, tiled=True)]
    pallas_call x0 -> x3, Pallas kernels: none -> 71 us  [the longest x2 48.3 us: local(): middle(*pieces[index], up, down, up_right, down_left, lows[index])]
    all_gather x0 -> x1, waiting for transfers between devices: none -> 45.8 us  [shared_sum(): return lax.all_gather(piece.astype(jnp.bfloat16), 'mp', axis=0, tiled=True)]
    all_gather x0 -> x2, blocking collectives: none -> 41 us  [shared_sum(): return lax.all_gather(piece.astype(jnp.bfloat16), 'mp', axis=0, tiled=True)]
    reshape x4 -> x2, local copies, waits for them, and re-layouts: 41.1 us -> 4.83 us  [local(): mixed = mixed.reshape(2, feat_width, part)]
    convert_element_type x2 -> x5, other arithmetic: 35.6 us -> 5.56 us  [the longest x3 3.27 us: shared_sum(): return lax.all_gather(piece.astype(jnp.bfloat16), 'mp', axis=0, tiled=True)]
  transfers between devices with their start and end apart: 16 -> 20, of which waited for: 3 -> 8; matrix products, arithmetic and copies ran while one was open for 41% -> 6% of each run, Pallas kernels for 0% -> 18%
where the time goes in v1:
time: 391 us
  waiting for transfers between devices  199 us (51%)
  Pallas kernels  71 us (18%)
  blocking collectives  41 us (10%)
  local copies, waits for them, and re-layouts  22 us (6%)
  other arithmetic  18.9 us (5%)
  starting transfers between devices  14.4 us (4%)
  between operations  14 us (4%)
  matrix products  9.89 us (3%)
    reduce_scatter x3, waiting for transfers between devices, shared_sum(): piece = lax.psum_scatter(total, 'mp', scatter_dimension=0, tiled=True)  96.2 us
    ppermute x16, waiting for transfers between devices, partner(): return lax.ppermute(block, axis, route)  57.3 us
    pallas_call x2, Pallas kernels, local(): middle(*pieces[index], up, down, up_right, down_left, lows[index])  48.3 us
    all_gather x1, waiting for transfers between devices, shared_sum(): return lax.all_gather(piece.astype(jnp.bfloat16), 'mp', axis=0, tiled=True)  45.8 us
    all_gather x2, blocking collectives, shared_sum(): return lax.all_gather(piece.astype(jnp.bfloat16), 'mp', axis=0, tiled=True)  41 us
    pallas_call x1, Pallas kernels, local(): pl.pallas_call(functools.partial(grad_kernel, CHUNKS, slots), grid=(col_c...  22.7 us
    ppermute x16, starting transfers between devices, partner(): return lax.ppermute(block, axis, route)  14.1 us
    unnamed x52, local copies, waits for them, and re-layouts  11.9 us
  transfers between devices with their start and end apart: 20, of which 8 were waited for; matrix products, arithmetic and copies ran while one was open for 6% of the time, Pallas kernels for 18%

profile of v1, /device:TPU:0, one launch (start us, length us, event | category | flops | bytes accessed | tf_op | source)
XLA Modules:
  0.0 390.7 jit_solution(9066101299358646193)
XLA Ops:
  11.9 64.8 %reduce-scatter.4.cloned.1.call-done = f32[32,1024]{1,0:T(8,128)} async-done(((f32[512,1024]{1,0:T(8,128)}), f32[32,1024]{1,0:T(8,128)}) %reduce-scatter.4.cloned.1.call-update) | async-done | bytes 131088 | tf_op jit(solution)/shard_map/reduce_scatter | solution.py:129
  79.5 2.3 copy.18
  85.7 2.3 collective-permute-start.3
  88.0 45.8 %all-gather.2.cloned.1.call-done = bf16[512,1024]{1,0:T(8,128)(2,1)} async-done(((bf16[32,1024]{1,0:T(8,128)(2,1)}), bf16[512,1024]{1,0:T(8,128)(2,1)}) %all-gather.2.cloned.1.call-update) | async-done | bytes 1048592 | tf_op jit(solution)/shard_map/all_gather | solution.py:130
  135.1 20.0 %collective-permute-done.11.refs_7_.refs_15_ = bf16[2,8,64,512]{3,2,1,0:T(8,128)(2,1)} collective-permute-done((bf16[2,8,64,512]{3,2,1,0:T(8,128)(2,1)}, bf16[2,8,64,512]{3,2,1,0:T(8,128)(2,1)}, u32[]{:S(2)}, u32[]{:S(2)}) %collective-permute-start.11) | collective-permute-done | bytes 1048608 | tf_op jit(solution)/shard_map/ppermute | solution.py:22
  155.1 1.8 collective-permute-start.1
  156.9 24.1 %shard_map.144 = (bf16[8,512,512]{2,1,0:T(8,128)(2,1)}, bf16[8,512,512]{2,1,0:T(8,128)(2,1)}, f32[2,8,64,512]{3,2,1,0:T(8,128)}, f32[512,512]{1,0:T(8,128)}, bf1...) custom-call(bf16[2,8,64,512]{3,2,1,0:T(8,128)(2,1)} %bitcast.13.refs, ...), custom_call_target="tpu_custom_call" | custom-call | flops 12884901888 | bytes 16777216 | tf_op jit(solution)/shard_map/pallas_call | solution.py:187
  185.2 2.6 collective-permute-start.12
  187.8 4.1 %collective-permute-done.2.refs_6_ = bf16[2,8,64,512]{3,2,1,0:T(8,128)(2,1)S(1)} collective-permute-done((bf16[2,8,64,512]{3,2,1,0:T(8,128)(2,1)S(1)}, bf16[2,8,64,512]{3,2,1,0:T(8,128)(2,1)S(1)}, u32[]{:S(2)}, u32[]{:S(2)}) %collective-permute-start.2) | collective-permute-done | bytes 1048608 | tf_op jit(solution)/shard_map/ppermute | solution.py:22
  191.9 1.8 collective-permute-start.14
  193.7 24.2 %shard_map.143 = (bf16[8,512,512]{2,1,0:T(8,128)(2,1)}, bf16[8,512,512]{2,1,0:T(8,128)(2,1)}, f32[2,8,64,512]{3,2,1,0:T(8,128)}, f32[512,512]{1,0:T(8,128)}, bf1...) custom-call(bf16[2,8,64,512]{3,2,1,0:T(8,128)(2,1)} %bitcast.58, ...), custom_call_target="tpu_custom_call" | custom-call | flops 12884901888 | bytes 16777216 | tf_op jit(solution)/shard_map/pallas_call | solution.py:187
  221.1 18.1 %collective-permute-done.12 = bf16[2,8,64,512]{3,2,1,0:T(8,128)(2,1)} collective-permute-done((bf16[2,8,64,512]{3,2,1,0:T(8,128)(2,1)}, bf16[2,8,64,512]{3,2,1,0:T(8,128)(2,1)}, u32[]{:S(2)}, u32[]{:S(2)}) %collective-permute-start.12) | collective-permute-done | bytes 1048608 | tf_op jit(solution)/shard_map/ppermute | solution.py:22
  239.3 2.0 collective-permute-start.6
  242.5 22.7 %shard_map.145 = (f32[8,512,512]{2,1,0:T(8,128)}, f32[8,512,512]{2,1,0:T(8,128)}, f32[256,4096]{1,0:T(8,128)}, f32[4096,256]{1,0:T(8,128)}) custom-call(bf16[2,8,64,512]{3,2,1,0:T(8,128)(2,1)S(1)} %bitcast.62, bf16[2,8,64,512]{3,2,1,0:T(8,128)(2,1)S(1)} %bitcast.63, bf16[2,8,64,512]{3,2,1,0:T(8,128)(2,1)S(1)} %bitcast.64, ...), custom_call_target="tpu_custom_call" | custom-call | flops 12884901888 | bytes 67108864 | tf_op jit(solution)/shard_map/pallas_call | solution.py:198
  265.3 4.3 %convert_add_fusion = f32[2,8,64,512]{3,2,1,0:T(8,128)} fusion(bf16[2,8,64,512]{3,2,1,0:T(8,128)(2,1)} %collective-permute-done.15, bf16[2,8,64,512]{3,2,1,0:T(8,128)(2,1)} %collective-permute-done.14, bf16[2,8,64,512]{3,2,1,0:T(8,128)(2,1)} %collective-permute-done.13, f32[2,8,64,512]{3,2,1,0:T(8,128)S(1)} %copy-done.24, ...), kind=kLoop, calls=%fused_computation.9 | loop fusion | flops 4194304 | bytes 8388608 | tf_op jit(solution)/shard_map/add | solution.py:219
  269.6 1.9 copy.19
  271.5 13.9 %collective-permute-done.4 = bf16[2,8,64,512]{3,2,1,0:T(8,128)(2,1)} collective-permute-done((bf16[2,8,64,512]{3,2,1,0:T(8,128)(2,1)}, bf16[2,8,64,512]{3,2,1,0:T(8,128)(2,1)}, u32[]{:S(2)}, u32[]{:S(2)}) %collective-permute-start.4) | collective-permute-done | bytes 1048608 | tf_op jit(solution)/shard_map/ppermute | solution.py:22
  286.7 5.0 %convert_add_fusion.1 = f32[2,8,64,512]{3,2,1,0:T(8,128)} fusion(bf16[2,8,64,512]{3,2,1,0:T(8,128)(2,1)} %collective-permute-done.7, bf16[2,8,64,512]{3,2,1,0:T(8,128)(2,1)} %collective-permute-done.6, bf16[2,8,64,512]{3,2,1,0:T(8,128)(2,1)} %collective-permute-done.5, f32[2,8,64,512]{3,2,1,0:T(8,128)} %get-tuple-element.28, ...), kind=kLoop, calls=%fused_computation.10 | loop fusion | flops 4194304 | bytes 8388608 | tf_op jit(solution)/shard_map/add | solution.py:219
  291.6 2.9 copy.17
  295.4 20.3 %all_gather.11 = bf16[512,512]{1,0:T(8,128)(2,1)S(1)} all-gather(bf16[32,512]{1,0:T(8,128)(2,1)S(1)} %convert_element_type.50), channel_id=1, replica_groups=mesh['groups'=2,'mp'=16] {'mp'}, dimensions={0}, use_global_device_ids=true | all-gather | bytes 557056 | tf_op jit(solution)/shard_map/all_gather | solution.py:130
  318.3 31.4 %reduce-scatter.6.cloned.1.call-done = f32[32,512]{1,0:T(8,128)} async-done(((f32[512,512]{1,0:T(8,128)}), f32[32,512]{1,0:T(8,128)}) %reduce-scatter.6.cloned.1.call-update) | async-done | bytes 65552 | tf_op jit(solution)/shard_map/reduce_scatter | solution.py:129
  350.5 20.8 %all_gather.10 = bf16[512,512]{1,0:T(8,128)(2,1)S(1)} all-gather(bf16[32,512]{1,0:T(8,128)(2,1)S(1)} %convert_element_type.44), channel_id=1, replica_groups=mesh['groups'=2,'mp'=16] {'mp'}, dimensions={0}, use_global_device_ids=true | all-gather | bytes 557056 | tf_op jit(solution)/shard_map/all_gather | solution.py:130
  377.7 2.0 copy.20
  379.7 1.7 fusion.1
  (101 shorter events, 36.0 us)
Async XLA Ops:
  7.2 69.5 %reduce-scatter.4.cloned.1.call-start = ((), (), s32[]{:S(2)}) async-start(), calls=%async_computation.3 | async-start | bytes 2228224 | tf_op jit(solution)/shard_map/reduce_scatter | solution.py:129
  11.8 66.5 %copy-start.14 = (bf16[1024,512]{1,0:T(8,128)(2,1)S(1)}, bf16[1024,512]{1,0:T(8,128)(2,1)}, u32[]{:S(2)}) copy-start(bf16[1024,512]{1,0:T(8,128)(2,1)} %param.8) | copy-start | bytes 3145732
  11.8 122.1 %all-gather.2.cloned.1.call-start = ((), (), s32[]{:S(2)}) async-start(), calls=%async_computation.4 | async-start | bytes 1114112 | tf_op jit(solution)/shard_map/all_gather | solution.py:130
  78.2 216.3 %reduce-scatter.8.cloned.1.call-start = ((), (), s32[]{:S(2)}) async-start(), calls=%async_computation.6 | async-start | bytes 1114112 | tf_op jit(solution)/shard_map/reduce_scatter | solution.py:129
  81.7 73.4 %collective-permute-start.11 = (bf16[2,8,64,512]{3,2,1,0:T(8,128)(2,1)}, bf16[2,8,64,512]{3,2,1,0:T(8,128)(2,1)}, u32[]{:S(2)}, u32[]{:S(2)}) collective-permute-start(bf16[2,8,64,512]{3,2,1,0:T(8,128)(2,1)} %bitcast.13.refs_0_.refs_1_.refs_2_.refs_3_.refs_8_.refs_9_.refs_10_.refs_11_), channel_id=1, source_target_pairs={{0,8},{8,0},{1,9},{9,1},{2,10},{10,2},{3,11},{11,3},{4,12},{12,4},... | collective-permute-start | bytes 3145736 | tf_op jit(solution)/shard_map/ppermute | solution.py:22
  83.2 71.9 %collective-permute-start.10 = (bf16[2,8,64,512]{3,2,1,0:T(8,128)(2,1)}, bf16[2,8,64,512]{3,2,1,0:T(8,128)(2,1)}, u32[]{:S(2)}, u32[]{:S(2)}) collective-permute-start(bf16[2,8,64,512]{3,2,1,0:T(8,128)(2,1)} %bitcast.13.refs_0_.refs_1_.refs_2_.refs_3_.refs_8_.refs_9_.refs_10_.refs_11_), channel_id=1, source_target_pairs={{0,4},{4,0},{1,5},{5,1},{2,6},{6,2},{3,7},{7,3},{8,12},{12,8},{9,1... | collective-permute-start | bytes 3145736 | tf_op jit(solution)/shard_map/ppermute | solution.py:22
  84.5 72.4 %collective-permute-start.9 = (bf16[2,8,64,512]{3,2,1,0:T(8,128)(2,1)}, bf16[2,8,64,512]{3,2,1,0:T(8,128)(2,1)}, u32[]{:S(2)}, u32[]{:S(2)}) collective-permute-start(bf16[2,8,64,512]{3,2,1,0:T(8,128)(2,1)} %bitcast.13.refs_0_.refs_1_.refs_2_.refs_3_.refs_8_.refs_9_.refs_10_.refs_11_), channel_id=1, source_target_pairs={{0,2},{2,0},{1,3},{3,1},{4,6},{6,4},{5,7},{7,5},{8,10},{10,8},{9,1... | collective-permute-start | bytes 3145736 | tf_op jit(solution)/shard_map/ppermute | solution.py:22
  85.2 71.7 %collective-permute-start.8 = (bf16[2,8,64,512]{3,2,1,0:T(8,128)(2,1)}, bf16[2,8,64,512]{3,2,1,0:T(8,128)(2,1)}, u32[]{:S(2)}, u32[]{:S(2)}) collective-permute-start(bf16[2,8,64,512]{3,2,1,0:T(8,128)(2,1)} %bitcast.13.refs_0_.refs_1_.refs_2_.refs_3_.refs_8_.refs_9_.refs_10_.refs_11_), channel_id=1, source_target_pairs={{0,1},{1,0},{2,3},{3,2},{4,5},{5,4},{6,7},{7,6},{8,9},{9,8},{10,11... | collective-permute-start | bytes 3145736 | tf_op jit(solution)/shard_map/ppermute | solution.py:22
  85.7 95.3 %copy-start.1 = (bf16[2,512,512]{2,1,0:T(8,128)(2,1)}, bf16[2,512,512]{2,1,0:T(8,128)(2,1)S(1)}, u32[]{:S(2)}) copy-start(bf16[2,512,512]{2,1,0:T(8,128)(2,1)S(1)} %copy.16) | copy-start | bytes 3145732
  85.7 102.1 %collective-permute-start.3 = (bf16[2,8,64,512]{3,2,1,0:T(8,128)(2,1)S(1)}, bf16[2,8,64,512]{3,2,1,0:T(8,128)(2,1)}, u32[]{:S(2)}, u32[]{:S(2)}) collective-permute-start(bf16[2,8,64,512]{3,2,1,0:T(8,128)(2,1)S(1)} %bitcast.54), channel_id=1, source_target_pairs={{0,8},{8,0},{1,9},{9,1},{2,10},{10,2},{3,11},{11,3},{4,12},{12,4},... | collective-permute-start | bytes 3145736 | tf_op jit(solution)/shard_map/ppermute | solution.py:22
  155.1 36.8 %collective-permute-start.2 = (bf16[2,8,64,512]{3,2,1,0:T(8,128)(2,1)S(1)}, bf16[2,8,64,512]{3,2,1,0:T(8,128)(2,1)S(1)}, u32[]{:S(2)}, u32[]{:S(2)}) collective-permute-start(bf16[2,8,64,512]{3,2,1,0:T(8,128)(2,1)S(1)} %bitcast.55), channel_id=1, source_target_pairs={{0,4},{4,0},{1,5},{5,1},{2,6},{6,2},{3,7},{7,3},{8,12},{12,8},{9,1... | collective-permute-start | bytes 3145736 | tf_op jit(solution)/shard_map/ppermute | solution.py:22
  155.1 38.6 %collective-permute-start.1 = (bf16[2,8,64,512]{3,2,1,0:T(8,128)(2,1)S(1)}, bf16[2,8,64,512]{3,2,1,0:T(8,128)(2,1)}, u32[]{:S(2)}, u32[]{:S(2)}) collective-permute-start(bf16[2,8,64,512]{3,2,1,0:T(8,128)(2,1)S(1)} %bitcast.56), channel_id=1, source_target_pairs={{0,2},{2,0},{1,3},{3,1},{4,6},{6,4},{5,7},{7,5},{8,10},{10,8},{9,1... | collective-permute-start | bytes 3145736 | tf_op jit(solution)/shard_map/ppermute | solution.py:22
  156.9 36.8 %collective-permute-start = (bf16[2,8,64,512]{3,2,1,0:T(8,128)(2,1)S(1)}, bf16[2,8,64,512]{3,2,1,0:T(8,128)(2,1)}, u32[]{:S(2)}, u32[]{:S(2)}) collective-permute-start(bf16[2,8,64,512]{3,2,1,0:T(8,128)(2,1)S(1)} %bitcast.57), channel_id=1, source_target_pairs={{0,1},{1,0},{2,3},{3,2},{4,5},{5,4},{6,7},{7,6},{8,9},{9,8},{10,11... | collective-permute-start | bytes 3145736 | tf_op jit(solution)/shard_map/ppermute | solution.py:22
  185.0 164.7 %reduce-scatter.6.cloned.1.call-start = ((), (), s32[]{:S(2)}) async-start(), calls=%async_computation.5 | async-start | bytes 1114112 | tf_op jit(solution)/shard_map/reduce_scatter | solution.py:129
  185.2 54.1 %collective-permute-start.12 = (bf16[2,8,64,512]{3,2,1,0:T(8,128)(2,1)}, bf16[2,8,64,512]{3,2,1,0:T(8,128)(2,1)}, u32[]{:S(2)}, u32[]{:S(2)}) collective-permute-start(bf16[2,8,64,512]{3,2,1,0:T(8,128)(2,1)} %copy-done.11), channel_id=1, source_target_pairs={{0,8},{8,0},{1,9},{9,1},{2,10},{10,2},{3,11},{11,3},{4,12},{12,4},... | collective-permute-start | bytes 3145736 | tf_op jit(solution)/shard_map/ppermute | solution.py:22
  187.8 51.5 %collective-permute-start.13 = (bf16[2,8,64,512]{3,2,1,0:T(8,128)(2,1)}, bf16[2,8,64,512]{3,2,1,0:T(8,128)(2,1)}, u32[]{:S(2)}, u32[]{:S(2)}) collective-permute-start(bf16[2,8,64,512]{3,2,1,0:T(8,128)(2,1)} %copy-done.10), channel_id=1, source_target_pairs={{0,4},{4,0},{1,5},{5,1},{2,6},{6,2},{3,7},{7,3},{8,12},{12,8},{9,1... | collective-permute-start | bytes 3145736 | tf_op jit(solution)/shard_map/ppermute | solution.py:22
  191.9 49.3 %collective-permute-start.14 = (bf16[2,8,64,512]{3,2,1,0:T(8,128)(2,1)}, bf16[2,8,64,512]{3,2,1,0:T(8,128)(2,1)}, u32[]{:S(2)}, u32[]{:S(2)}) collective-permute-start(bf16[2,8,64,512]{3,2,1,0:T(8,128)(2,1)} %copy-done.7), channel_id=1, source_target_pairs={{0,2},{2,0},{1,3},{3,1},{4,6},{6,4},{5,7},{7,5},{8,10},{10,8},{9,1... | collective-permute-start | bytes 3145736 | tf_op jit(solution)/shard_map/ppermute | solution.py:22
  193.7 71.5 %collective-permute-start.15 = (bf16[2,8,64,512]{3,2,1,0:T(8,128)(2,1)}, bf16[2,8,64,512]{3,2,1,0:T(8,128)(2,1)}, u32[]{:S(2)}, u32[]{:S(2)}) collective-permute-start(bf16[2,8,64,512]{3,2,1,0:T(8,128)(2,1)} %copy-done.5), channel_id=1, source_target_pairs={{0,1},{1,0},{2,3},{3,2},{4,5},{5,4},{6,7},{7,6},{8,9},{9,8},{10,11... | collective-permute-start | bytes 3145736 | tf_op jit(solution)/shard_map/ppermute | solution.py:22
  193.7 47.5 %copy-start.2 = (bf16[2,512,512]{2,1,0:T(8,128)(2,1)S(1)}, bf16[2,512,512]{2,1,0:T(8,128)(2,1)}, u32[]{:S(2)}) copy-start(bf16[2,512,512]{2,1,0:T(8,128)(2,1)} %copy-done.1) | copy-start | bytes 3145732
  220.9 64.5 %collective-permute-start.4 = (bf16[2,8,64,512]{3,2,1,0:T(8,128)(2,1)}, bf16[2,8,64,512]{3,2,1,0:T(8,128)(2,1)}, u32[]{:S(2)}, u32[]{:S(2)}) collective-permute-start(bf16[2,8,64,512]{3,2,1,0:T(8,128)(2,1)} %get-tuple-element.29), channel_id=1, source_target_pairs={{0,8},{8,0},{1,9},{9,1},{2,10},{10,2},{3,11},{11,3},{4,12},{12,4},... | collective-permute-start | bytes 3145736 | tf_op jit(solution)/shard_map/ppermute | solution.py:22
  239.3 47.4 %collective-permute-start.5 = (bf16[2,8,64,512]{3,2,1,0:T(8,128)(2,1)}, bf16[2,8,64,512]{3,2,1,0:T(8,128)(2,1)}, u32[]{:S(2)}, u32[]{:S(2)}) collective-permute-start(bf16[2,8,64,512]{3,2,1,0:T(8,128)(2,1)} %copy-done.9), channel_id=1, source_target_pairs={{0,4},{4,0},{1,5},{5,1},{2,6},{6,2},{3,7},{7,3},{8,12},{12,8},{9,1... | collective-permute-start | bytes 3145736 | tf_op jit(solution)/shard_map/ppermute | solution.py:22
  239.3 47.4 %collective-permute-start.6 = (bf16[2,8,64,512]{3,2,1,0:T(8,128)(2,1)}, bf16[2,8,64,512]{3,2,1,0:T(8,128)(2,1)}, u32[]{:S(2)}, u32[]{:S(2)}) collective-permute-start(bf16[2,8,64,512]{3,2,1,0:T(8,128)(2,1)} %copy-done.8), channel_id=1, source_target_pairs={{0,2},{2,0},{1,3},{3,1},{4,6},{6,4},{5,7},{7,5},{8,10},{10,8},{9,1... | collective-permute-start | bytes 3145736 | tf_op jit(solution)/shard_map/ppermute | solution.py:22
  241.3 45.4 %collective-permute-start.7 = (bf16[2,8,64,512]{3,2,1,0:T(8,128)(2,1)}, bf16[2,8,64,512]{3,2,1,0:T(8,128)(2,1)}, u32[]{:S(2)}, u32[]{:S(2)}) collective-permute-start(bf16[2,8,64,512]{3,2,1,0:T(8,128)(2,1)} %copy-done.6), channel_id=1, source_target_pairs={{0,1},{1,0},{2,3},{3,2},{4,5},{5,4},{6,7},{7,6},{8,9},{9,8},{10,11... | collective-permute-start | bytes 3145736 | tf_op jit(solution)/shard_map/ppermute | solution.py:22
  317.0 55.5 %copy-start.13 = (bf16[1024,512]{1,0:T(8,128)(2,1)S(1)}, bf16[1024,512]{1,0:T(8,128)(2,1)}, u32[]{:S(2)}) copy-start(bf16[1024,512]{1,0:T(8,128)(2,1)} %param.15) | copy-start | bytes 3145732
  (21 other events, 79.1 us)
Sparse Core Ops, SparseCore 0:
  12.3 64.2 reduce-scatter.3
  79.6 54.2 all-gather.1
  185.1 103.9 reduce-scatter.7
  292.6 57.0 reduce-scatter.5

commit v2 on v1

--- a/solution.py
+++ b/solution.py
@@ -125,8 +125,15 @@
         for start in range(0, tok_rows, part)
     ]
 
-    def shared_sum(total):
+    fars = [
+        [partner(mine[index], "mp", level) for level in reversed(range(remote_bits))][::-1]
+        for index in range(CHUNKS)
+    ]
+
+    def shared_sum(total, after=()):
         piece = lax.psum_scatter(total, "mp", scatter_dimension=0, tiled=True)
+        for other in after:
+            piece = piece + 0.0 * other[0, 0, :1, :1].astype(jnp.float32)
         return lax.all_gather(piece.astype(jnp.bfloat16), "mp", axis=0, tiled=True)
 
     low = shared_sum(
@@ -135,7 +142,8 @@
                 jnp.einsum("dr,dt->rt", up_left, both[0], preferred_element_type=jnp.float32),
                 jnp.einsum("rd,dt->rt", down_right, both[1], preferred_element_type=jnp.float32),
             ]
-        )
+        ),
+        fars[0],
     )
     lows = [low[:, start : start + part] for start in range(0, tok_rows, part)]
 
@@ -181,8 +189,7 @@
     )
     pieces, fields, grads, nears, sums, far_terms = [], [], [], [], [], []
     for index in range(CHUNKS):
-        far = [partner(mine[index], "mp", level) for level in reversed(range(remote_bits))][::-1]
-        pieces.append([mine[index]] * (1 + local_bits) + far)
+        pieces.append([mine[index]] * (1 + local_bits) + fars[index])
     for index in range(CHUNKS):
         act, grad, near, total, *terms = middle(
             *pieces[index], up, down, up_right, down_left, lows[index]
@@ -190,7 +197,7 @@
         far_terms.append(
             [partner(terms[level], "mp", level) for level in reversed(range(remote_bits))]
         )
-        sums.append(shared_sum(total))
+        sums.append(total)
         fields.append(act)
         grads.append(grad)
         nears.append(near)
@@ -212,6 +219,8 @@
         ),
     )(*[piece for group in pieces for piece in group], *fields, *grads, *lows)
 
+    total = shared_sum(jnp.concatenate(sums, axis=1))
+    sums = [total[:, start : start + part] for start in range(0, tok_rows, part)]
     results = []
     for index in range(CHUNKS):
         mixed = nears[index]
@@ -230,7 +239,6 @@
         )
         results.append((mixed + back).astype(jnp.bfloat16))
     result = jnp.concatenate(results, axis=2)
-    total = jnp.concatenate(sums, axis=1)
     grad_down_right = jnp.einsum(
         "rt,dt->rd", total[:rank], both[1], preferred_element_type=jnp.float32
     )

time: 391 us -> 376 us (0.962)
  blocking collectives: 41 us -> 0 us
  waiting for transfers between devices: 199 us -> 216 us
  local copies, waits for them, and re-layouts: 22 us -> 26.8 us
    all_gather x2 -> x0, blocking collectives: 41 us -> none  [shared_sum(): return lax.all_gather(piece.astype(jnp.bfloat16), 'mp', axis=0, tiled=True)]
    reduce_scatter x3 -> x2, waiting for transfers between devices: 96.2 us -> 116 us  [shared_sum(): piece = lax.psum_scatter(total, 'mp', scatter_dimension=0, tiled=True)]
    ppermute x16, waiting for transfers between devices: 57.3 us -> 51.1 us  [partner(): return lax.ppermute(block, axis, route)]
    unnamed x52 -> x55, local copies, waits for them, and re-layouts: 11.9 us -> 15.7 us
    all_gather x1 -> x2, waiting for transfers between devices: 45.8 us -> 49.1 us  [shared_sum(): return lax.all_gather(piece.astype(jnp.bfloat16), 'mp', axis=0, tiled=True)]
  transfers between devices with their start and end apart: 20 -> 20, of which waited for: 8 -> 4; matrix products, arithmetic and copies ran while one was open for 6% -> 6% of each run, Pallas kernels for 18% -> 12%
where the time goes in v2:
time: 376 us; the launch traced here: 375 us
  waiting for transfers between devices  216 us (57%)
  Pallas kernels  70.7 us (19%)
  local copies, waits for them, and re-layouts  26.8 us (7%)
  other arithmetic  19.1 us (5%)
  starting transfers between devices  16.9 us (4%)
  between operations  16.8 us (4%)
  matrix products  9.13 us (2%)
    reduce_scatter x2, waiting for transfers between devices, shared_sum(): piece = lax.psum_scatter(total, 'mp', scatter_dimension=0, tiled=True)  116 us
    ppermute x16, waiting for transfers between devices, partner(): return lax.ppermute(block, axis, route)  51.1 us
    all_gather x2, waiting for transfers between devices, shared_sum(): return lax.all_gather(piece.astype(jnp.bfloat16), 'mp', axis=0, tiled=True)  49.1 us
    pallas_call x2, Pallas kernels, local(): middle(*pieces[index], up, down, up_right, down_left, lows[index])  47.9 us
    pallas_call x1, Pallas kernels, local(): pl.pallas_call(functools.partial(grad_kernel, CHUNKS, slots), grid=(col_c...  22.8 us
    ppermute x16, starting transfers between devices, partner(): return lax.ppermute(block, axis, route)  16.5 us
    unnamed x55, local copies, waits for them, and re-layouts  15.7 us
    add x2, other arithmetic, local(): mixed = mixed + term.astype(jnp.float32)  9.29 us
  transfers between devices with their start and end apart: 20, of which 4 were waited for; matrix products, arithmetic and copies ran while one was open for 6% of the time, Pallas kernels for 12%

profile of v2, /device:TPU:0, one launch (start us, length us, event | category | flops | bytes accessed | tf_op | source)
XLA Modules:
  0.0 375.3 jit_solution(7481074836260412999)
XLA Ops:
  8.1 1.7 fusion.14
  14.7 4.1 %collective-permute-start.3 = (bf16[2,8,64,512]{3,2,1,0:T(8,128)(2,1)S(1)}, bf16[2,8,64,512]{3,2,1,0:T(8,128)(2,1)S(1)}, u32[]{:S(2)}, u32[]{:S(2)}) collective-permute-start(bf16[2,8,64,512]{3,2,1,0:T(8,128)(2,1)S(1)} %bitcast.58), channel_id=1, source_target_pairs={{0,8},{8,0},{1,9},{9,1},{2,10},{10,2},{3,11},{11,3},{4,12},{12,4},... | collective-permute-start | bytes 3145736 | tf_op jit(solution)/shard_map/ppermute | solution.py:22
  18.8 1.6 collective-permute-start.2
  20.4 1.5 collective-permute-start.1
  21.9 51.1 %collective-permute-done.3.refs_7_ = bf16[2,8,64,512]{3,2,1,0:T(8,128)(2,1)S(1)} collective-permute-done((bf16[2,8,64,512]{3,2,1,0:T(8,128)(2,1)S(1)}, bf16[2,8,64,512]{3,2,1,0:T(8,128)(2,1)S(1)}, u32[]{:S(2)}, u32[]{:S(2)}) %collective-permute-start.3) | collective-permute-done | bytes 1048608 | tf_op jit(solution)/shard_map/ppermute | solution.py:22
  78.8 12.5 %reduce-scatter.3.cloned.1.call-done = f32[32,1024]{1,0:T(8,128)} async-done(((f32[512,1024]{1,0:T(8,128)}), f32[32,1024]{1,0:T(8,128)}) %reduce-scatter.3.cloned.1.call-update) | async-done | bytes 131088 | tf_op jit(solution)/shard_map/reduce_scatter | solution.py:134
  91.3 1.6 add_convert_fusion
  92.9 2.3 copy.17
  95.2 1.5 collective-permute-start.11
  98.6 49.1 %all-gather.3.cloned.1.call-done = bf16[512,1024]{1,0:T(8,128)(2,1)} async-done(((bf16[32,1024]{1,0:T(8,128)(2,1)}), bf16[512,1024]{1,0:T(8,128)(2,1)}) %all-gather.3.cloned.1.call-update) | async-done | bytes 1048592 | tf_op jit(solution)/shard_map/all_gather | solution.py:137
  149.1 24.0 %shard_map.143 = (bf16[8,512,512]{2,1,0:T(8,128)(2,1)}, bf16[8,512,512]{2,1,0:T(8,128)(2,1)}, f32[2,8,64,512]{3,2,1,0:T(8,128)}, f32[512,512]{1,0:T(8,128)S(1)},...) custom-call(bf16[2,8,64,512]{3,2,1,0:T(8,128)(2,1)} %bitcast.62, ...), custom_call_target="tpu_custom_call" | custom-call | flops 12884901888 | bytes 16777216 | tf_op jit(solution)/shard_map/pallas_call | solution.py:194
  177.1 23.9 %shard_map.144 = (bf16[8,512,512]{2,1,0:T(8,128)(2,1)}, bf16[8,512,512]{2,1,0:T(8,128)(2,1)}, f32[2,8,64,512]{3,2,1,0:T(8,128)}, f32[512,512]{1,0:T(8,128)S(1)},...) custom-call(bf16[2,8,64,512]{3,2,1,0:T(8,128)(2,1)} %bitcast.78, ...), custom_call_target="tpu_custom_call" | custom-call | flops 12884901888 | bytes 16777216 | tf_op jit(solution)/shard_map/pallas_call | solution.py:194
  204.9 1.5 pad_maximum_fusion.1
  206.7 1.9 collective-permute-start.12
  208.6 3.0 collective-permute-start.13
  211.6 103.1 %reduce-scatter.5.cloned.1.call-done = f32[32,1024]{1,0:T(8,128)} async-done(((f32[512,1024]{1,0:T(8,128)}), f32[32,1024]{1,0:T(8,128)}) %reduce-scatter.5.cloned.1.call-update) | async-done | bytes 131088 | tf_op jit(solution)/shard_map/reduce_scatter | solution.py:134
  314.7 1.5 convert_element_type.61
  319.8 22.8 %shard_map.145 = (f32[8,512,512]{2,1,0:T(8,128)}, f32[8,512,512]{2,1,0:T(8,128)}, f32[256,4096]{1,0:T(8,128)}, f32[4096,256]{1,0:T(8,128)}) custom-call(bf16[2,8,64,512]{3,2,1,0:T(8,128)(2,1)S(1)} %bitcast.66, bf16[2,8,64,512]{3,2,1,0:T(8,128)(2,1)S(1)} %bitcast.67, bf16[2,8,64,512]{3,2,1,0:T(8,128)(2,1)S(1)} %bitcast.68, ...), custom_call_target="tpu_custom_call" | custom-call | flops 12884901888 | bytes 67108864 | tf_op jit(solution)/shard_map/pallas_call | solution.py:205
  342.6 4.3 %convert_add_fusion = f32[2,8,64,512]{3,2,1,0:T(8,128)} fusion(bf16[2,8,64,512]{3,2,1,0:T(8,128)(2,1)} %collective-permute-done.15, bf16[2,8,64,512]{3,2,1,0:T(8,128)(2,1)} %collective-permute-done.14, bf16[2,8,64,512]{3,2,1,0:T(8,128)(2,1)} %collective-permute-done.13, f32[2,8,64,512]{3,2,1,0:T(8,128)S(1)} %copy-done.25, ...), kind=kLoop, calls=%fused_computation.10 | loop fusion | flops 4194304 | bytes 8388608 | tf_op jit(solution)/shard_map/add | solution.py:228
  346.9 1.9 copy.19
  348.9 5.0 %convert_add_fusion.1 = f32[2,8,64,512]{3,2,1,0:T(8,128)} fusion(bf16[2,8,64,512]{3,2,1,0:T(8,128)(2,1)} %collective-permute-done.7, bf16[2,8,64,512]{3,2,1,0:T(8,128)(2,1)} %collective-permute-done.6, bf16[2,8,64,512]{3,2,1,0:T(8,128)(2,1)} %collective-permute-done.5, f32[2,8,64,512]{3,2,1,0:T(8,128)} %get-tuple-element.28, ...), kind=kLoop, calls=%fused_computation.11 | loop fusion | flops 4194304 | bytes 8388608 | tf_op jit(solution)/shard_map/add | solution.py:228
  353.9 3.0 copy.18
  356.9 2.3 convolution_bitcast_fusion.4
  359.1 2.1 copy.20
  (104 shorter events, 31.4 us)
Async XLA Ops:
  7.2 84.1 %reduce-scatter.3.cloned.1.call-start = ((), (), s32[]{:S(2)}) async-start(), calls=%async_computation.2 | async-start | bytes 2228224 | tf_op jit(solution)/shard_map/reduce_scatter | solution.py:134
  11.8 136.0 %all-gather.3.cloned.1.call-start = ((), (), s32[]{:S(2)}) async-start(), calls=%async_computation.3 | async-start | bytes 1114112 | tf_op jit(solution)/shard_map/all_gather | solution.py:137
  14.7 134.3 %copy-start.1 = (bf16[2,512,512]{2,1,0:T(8,128)(2,1)}, bf16[2,512,512]{2,1,0:T(8,128)(2,1)S(1)}, u32[]{:S(2)}) copy-start(bf16[2,512,512]{2,1,0:T(8,128)(2,1)S(1)} %copy.16) | copy-start | bytes 3145732
  14.7 58.3 %collective-permute-start.3 = (bf16[2,8,64,512]{3,2,1,0:T(8,128)(2,1)S(1)}, bf16[2,8,64,512]{3,2,1,0:T(8,128)(2,1)S(1)}, u32[]{:S(2)}, u32[]{:S(2)}) collective-permute-start(bf16[2,8,64,512]{3,2,1,0:T(8,128)(2,1)S(1)} %bitcast.58), channel_id=1, source_target_pairs={{0,8},{8,0},{1,9},{9,1},{2,10},{10,2},{3,11},{11,3},{4,12},{12,4},... | collective-permute-start | bytes 3145736 | tf_op jit(solution)/shard_map/ppermute | solution.py:22
  18.8 55.4 %collective-permute-start.2 = (bf16[2,8,64,512]{3,2,1,0:T(8,128)(2,1)S(1)}, bf16[2,8,64,512]{3,2,1,0:T(8,128)(2,1)S(1)}, u32[]{:S(2)}, u32[]{:S(2)}) collective-permute-start(bf16[2,8,64,512]{3,2,1,0:T(8,128)(2,1)S(1)} %bitcast.59), channel_id=1, source_target_pairs={{0,4},{4,0},{1,5},{5,1},{2,6},{6,2},{3,7},{7,3},{8,12},{12,8},{9,1... | collective-permute-start | bytes 3145736 | tf_op jit(solution)/shard_map/ppermute | solution.py:22
  20.4 55.0 %collective-permute-start.1 = (bf16[2,8,64,512]{3,2,1,0:T(8,128)(2,1)S(1)}, bf16[2,8,64,512]{3,2,1,0:T(8,128)(2,1)S(1)}, u32[]{:S(2)}, u32[]{:S(2)}) collective-permute-start(bf16[2,8,64,512]{3,2,1,0:T(8,128)(2,1)S(1)} %bitcast.60), channel_id=1, source_target_pairs={{0,2},{2,0},{1,3},{3,1},{4,6},{6,4},{5,7},{7,5},{8,10},{10,8},{9,1... | collective-permute-start | bytes 3145736 | tf_op jit(solution)/shard_map/ppermute | solution.py:22
  21.9 54.7 %collective-permute-start = (bf16[2,8,64,512]{3,2,1,0:T(8,128)(2,1)S(1)}, bf16[2,8,64,512]{3,2,1,0:T(8,128)(2,1)S(1)}, u32[]{:S(2)}, u32[]{:S(2)}) collective-permute-start(bf16[2,8,64,512]{3,2,1,0:T(8,128)(2,1)S(1)} %bitcast.61), channel_id=1, source_target_pairs={{0,1},{1,0},{2,3},{3,2},{4,5},{5,4},{6,7},{7,6},{8,9},{9,8},{10,11... | collective-permute-start | bytes 3145736 | tf_op jit(solution)/shard_map/ppermute | solution.py:22
  74.2 74.9 %copy-start.3 = (bf16[2,8,64,512]{3,2,1,0:T(8,128)(2,1)}, bf16[2,8,64,512]{3,2,1,0:T(8,128)(2,1)S(1)}, u32[]{:S(2)}) copy-start(bf16[2,8,64,512]{3,2,1,0:T(8,128)(2,1)S(1)} %collective-permute-done.2.refs_6_) | copy-start | bytes 3145732
  92.9 221.9 %reduce-scatter.5.cloned.1.call-start = ((), (), s32[]{:S(2)}) async-start(), calls=%async_computation.4 | async-start | bytes 2228224 | tf_op jit(solution)/shard_map/reduce_scatter | solution.py:134
  95.2 81.8 %collective-permute-start.11 = (bf16[2,8,64,512]{3,2,1,0:T(8,128)(2,1)}, bf16[2,8,64,512]{3,2,1,0:T(8,128)(2,1)}, u32[]{:S(2)}, u32[]{:S(2)}) collective-permute-start(bf16[2,8,64,512]{3,2,1,0:T(8,128)(2,1)} %bitcast.74), channel_id=1, source_target_pairs={{0,8},{8,0},{1,9},{9,1},{2,10},{10,2},{3,11},{11,3},{4,12},{12,4},... | collective-permute-start | bytes 3145736 | tf_op jit(solution)/shard_map/ppermute | solution.py:22
  96.7 80.4 %collective-permute-start.10 = (bf16[2,8,64,512]{3,2,1,0:T(8,128)(2,1)}, bf16[2,8,64,512]{3,2,1,0:T(8,128)(2,1)}, u32[]{:S(2)}, u32[]{:S(2)}) collective-permute-start(bf16[2,8,64,512]{3,2,1,0:T(8,128)(2,1)} %bitcast.75), channel_id=1, source_target_pairs={{0,4},{4,0},{1,5},{5,1},{2,6},{6,2},{3,7},{7,3},{8,12},{12,8},{9,1... | collective-permute-start | bytes 3145736 | tf_op jit(solution)/shard_map/ppermute | solution.py:22
  97.9 79.2 %collective-permute-start.9 = (bf16[2,8,64,512]{3,2,1,0:T(8,128)(2,1)}, bf16[2,8,64,512]{3,2,1,0:T(8,128)(2,1)}, u32[]{:S(2)}, u32[]{:S(2)}) collective-permute-start(bf16[2,8,64,512]{3,2,1,0:T(8,128)(2,1)} %bitcast.76), channel_id=1, source_target_pairs={{0,2},{2,0},{1,3},{3,1},{4,6},{6,4},{5,7},{7,5},{8,10},{10,8},{9,1... | collective-permute-start | bytes 3145736 | tf_op jit(solution)/shard_map/ppermute | solution.py:22
  98.6 78.4 %collective-permute-start.8 = (bf16[2,8,64,512]{3,2,1,0:T(8,128)(2,1)}, bf16[2,8,64,512]{3,2,1,0:T(8,128)(2,1)}, u32[]{:S(2)}, u32[]{:S(2)}) collective-permute-start(bf16[2,8,64,512]{3,2,1,0:T(8,128)(2,1)} %bitcast.77), channel_id=1, source_target_pairs={{0,1},{1,0},{2,3},{3,2},{4,5},{5,4},{6,7},{7,6},{8,9},{9,8},{10,11... | collective-permute-start | bytes 3145736 | tf_op jit(solution)/shard_map/ppermute | solution.py:22
  206.4 110.9 %copy-start.2 = (bf16[2,512,512]{2,1,0:T(8,128)(2,1)S(1)}, bf16[2,512,512]{2,1,0:T(8,128)(2,1)}, u32[]{:S(2)}) copy-start(bf16[2,512,512]{2,1,0:T(8,128)(2,1)} %copy-done.1) | copy-start | bytes 3145732
  206.4 110.9 %copy-start.4 = (bf16[2,8,64,512]{3,2,1,0:T(8,128)(2,1)S(1)}, bf16[2,8,64,512]{3,2,1,0:T(8,128)(2,1)}, u32[]{:S(2)}) copy-start(bf16[2,8,64,512]{3,2,1,0:T(8,128)(2,1)} %copy-done.3) | copy-start | bytes 3145732
  206.5 150.4 %all-gather.5.cloned.1.call-start = ((), (), s32[]{:S(2)}) async-start(), calls=%async_computation.5 | async-start | bytes 1114112 | tf_op jit(solution)/shard_map/all_gather | solution.py:137
  206.7 109.6 %collective-permute-start.12 = (bf16[2,8,64,512]{3,2,1,0:T(8,128)(2,1)}, bf16[2,8,64,512]{3,2,1,0:T(8,128)(2,1)}, u32[]{:S(2)}, u32[]{:S(2)}) collective-permute-start(bf16[2,8,64,512]{3,2,1,0:T(8,128)(2,1)} %copy-done.16), channel_id=1, source_target_pairs={{0,8},{8,0},{1,9},{9,1},{2,10},{10,2},{3,11},{11,3},{4,12},{12,4},... | collective-permute-start | bytes 3145736 | tf_op jit(solution)/shard_map/ppermute | solution.py:22
  208.6 107.8 %collective-permute-start.13 = (bf16[2,8,64,512]{3,2,1,0:T(8,128)(2,1)}, bf16[2,8,64,512]{3,2,1,0:T(8,128)(2,1)}, u32[]{:S(2)}, u32[]{:S(2)}) collective-permute-start(bf16[2,8,64,512]{3,2,1,0:T(8,128)(2,1)} %copy-done.15), channel_id=1, source_target_pairs={{0,4},{4,0},{1,5},{5,1},{2,6},{6,2},{3,7},{7,3},{8,12},{12,8},{9,1... | collective-permute-start | bytes 3145736 | tf_op jit(solution)/shard_map/ppermute | solution.py:22
  211.5 105.8 %collective-permute-start.14 = (bf16[2,8,64,512]{3,2,1,0:T(8,128)(2,1)}, bf16[2,8,64,512]{3,2,1,0:T(8,128)(2,1)}, u32[]{:S(2)}, u32[]{:S(2)}) collective-permute-start(bf16[2,8,64,512]{3,2,1,0:T(8,128)(2,1)} %copy-done.14), channel_id=1, source_target_pairs={{0,2},{2,0},{1,3},{3,1},{4,6},{6,4},{5,7},{7,5},{8,10},{10,8},{9,1... | collective-permute-start | bytes 3145736 | tf_op jit(solution)/shard_map/ppermute | solution.py:22
  211.5 131.0 %collective-permute-start.15 = (bf16[2,8,64,512]{3,2,1,0:T(8,128)(2,1)}, bf16[2,8,64,512]{3,2,1,0:T(8,128)(2,1)}, u32[]{:S(2)}, u32[]{:S(2)}) collective-permute-start(bf16[2,8,64,512]{3,2,1,0:T(8,128)(2,1)} %copy-done.13), channel_id=1, source_target_pairs={{0,1},{1,0},{2,3},{3,2},{4,5},{5,4},{6,7},{7,6},{8,9},{9,8},{10,11... | collective-permute-start | bytes 3145736 | tf_op jit(solution)/shard_map/ppermute | solution.py:22
  211.5 137.3 %collective-permute-start.4 = (bf16[2,8,64,512]{3,2,1,0:T(8,128)(2,1)}, bf16[2,8,64,512]{3,2,1,0:T(8,128)(2,1)}, u32[]{:S(2)}, u32[]{:S(2)}) collective-permute-start(bf16[2,8,64,512]{3,2,1,0:T(8,128)(2,1)} %copy-done.12), channel_id=1, source_target_pairs={{0,8},{8,0},{1,9},{9,1},{2,10},{10,2},{3,11},{11,3},{4,12},{12,4},... | collective-permute-start | bytes 3145736 | tf_op jit(solution)/shard_map/ppermute | solution.py:22
  316.3 32.5 %collective-permute-start.5 = (bf16[2,8,64,512]{3,2,1,0:T(8,128)(2,1)}, bf16[2,8,64,512]{3,2,1,0:T(8,128)(2,1)}, u32[]{:S(2)}, u32[]{:S(2)}) collective-permute-start(bf16[2,8,64,512]{3,2,1,0:T(8,128)(2,1)} %copy-done.11), channel_id=1, source_target_pairs={{0,4},{4,0},{1,5},{5,1},{2,6},{6,2},{3,7},{7,3},{8,12},{12,8},{9,1... | collective-permute-start | bytes 3145736 | tf_op jit(solution)/shard_map/ppermute | solution.py:22
  316.4 32.5 %collective-permute-start.6 = (bf16[2,8,64,512]{3,2,1,0:T(8,128)(2,1)}, bf16[2,8,64,512]{3,2,1,0:T(8,128)(2,1)}, u32[]{:S(2)}, u32[]{:S(2)}) collective-permute-start(bf16[2,8,64,512]{3,2,1,0:T(8,128)(2,1)} %copy-done.10), channel_id=1, source_target_pairs={{0,2},{2,0},{1,3},{3,1},{4,6},{6,4},{5,7},{7,5},{8,10},{10,8},{9,1... | collective-permute-start | bytes 3145736 | tf_op jit(solution)/shard_map/ppermute | solution.py:22
  317.3 31.5 %collective-permute-start.7 = (bf16[2,8,64,512]{3,2,1,0:T(8,128)(2,1)}, bf16[2,8,64,512]{3,2,1,0:T(8,128)(2,1)}, u32[]{:S(2)}, u32[]{:S(2)}) collective-permute-start(bf16[2,8,64,512]{3,2,1,0:T(8,128)(2,1)} %copy-done.9), channel_id=1, source_target_pairs={{0,1},{1,0},{2,3},{3,2},{4,5},{5,4},{6,7},{7,6},{8,9},{9,8},{10,11... | collective-permute-start | bytes 3145736 | tf_op jit(solution)/shard_map/ppermute | solution.py:22
  (23 other events, 83.4 us)
Sparse Core Ops, SparseCore 0:
  12.3 78.9 reduce-scatter.2
  94.3 53.4 all-gather.2
  206.6 108.1 reduce-scatter.4
  317.3 36.6 all-gather.4
